TPU v7x, 256 devices: a whole 4x4x8 slice. The times are simulated.
256 devices in a mesh: section: 2 (over y_lo), fsdp: 32 (over x, z), dp: 4 (over y_hi, core).
Axes of the slice: x: 4, y: 4 (y_hi: 2, y_lo: 2; y = y_hi * 2 + y_lo), z: 8, core: 2. Of those that a mesh axis runs over, the one named last changes fastest.
Arguments:
- activations: bfloat16 [2, 4, 4096, 3584], P('section', None, ('fsdp', 'dp')), may hold values from -6 to 6
- out_grad: bfloat16 [2, 4, 4096, 14336], P('section', None, ('fsdp', 'dp')), may hold values from -6 to 6
- blocks: bfloat16 [2, 128, 128, 128], P('section', 'fsdp'), may hold values from -0.5 to 0.5
- pattern: int32 [2, 128, 2], P('section', 'fsdp'), may hold values from 0 to 111, as said below
- order: int32 [4], replicated, may hold values from 0 to 3, each once
Outputs:
- received: bfloat16 [2, 4, 4096, 3584], P('section', None, ('fsdp', 'dp'))
- weight_grad: float32 [2, 128, 128, 128], P('section', 'fsdp')
Inputs may be any that keep to these rules, and one draw needn't show every extreme that they name: pattern[s, b, 0] < 28 and pattern[s, b, 1] < 112; no two blocks of one section share both indices; within a section the blocks stand in ascending order of (row, column). `order`: a permutation of the microbatches.
All inputs are finite; a program needn't handle non-finite values.
Results may differ from a plain program's by a relative error of at most 0.0049.
Values may be sent and summed in bfloat16 or wider, within the bound.
A program may use at most 128 MiB of HBM per device.

v0:
```python
import math
import jax
import jax.numpy as jnp
from jax import lax
from jax.sharding import PartitionSpec as P


def passed_along(block, axis, distance):
    devices = range(lax.axis_size(axis))
    route = [(i - distance, i) for i in devices if i - distance in devices]
    return lax.ppermute(block, axis, route)


def silu_slope(pre_act):
    sigmoid_val = jax.nn.sigmoid(pre_act)
    return sigmoid_val * (1.0 + pre_act * (1.0 - sigmoid_val))


def in_groups(step_fn, running, shard_blocks):
    block_count = shard_blocks.shape[0]
    group_size = math.gcd(block_count, 32)

    def one_group(number, carried):
        segment = lax.dynamic_slice_in_dim(shard_blocks, number * group_size, group_size, 0)
        return step_fn(carried, segment, number * group_size)

    return lax.fori_loop(0, block_count // group_size, one_group, running)


def local(activations, out_grad, blocks, pattern, order):
    block_size = blocks.shape[-1]
    micro_count = activations.shape[1]
    tok_rows = activations.shape[1] * activations.shape[2]
    row_count = activations.shape[3] // block_size
    col_count = out_grad.shape[3] // block_size
    features = activations[0].reshape(tok_rows, row_count, block_size)
    hidden_grad = out_grad[0].reshape(tok_rows, out_grad.shape[3])
    own_blocks = blocks[0]
    all_indices = lax.all_gather(pattern[0], "fsdp", axis=0, tiled=True)

    def forward_step(running, shard_blocks, first_block):
        indices = lax.dynamic_slice_in_dim(all_indices, first_block, shard_blocks.shape[0], 0)
        rows_in = jnp.take(features, indices[:, 0], axis=1)
        product = jnp.einsum(
            "tbk,bkn->tbn", rows_in, shard_blocks, preferred_element_type=jnp.float32
        )
        return running.at[:, indices[:, 1]].add(product)

    pre_zero = jnp.zeros((tok_rows, col_count, block_size), jnp.float32)
    pre_act = in_groups(
        forward_step, pre_zero, lax.all_gather(own_blocks, "fsdp", axis=0, tiled=True)
    )
    act_grad = (hidden_grad.astype(jnp.float32) * silu_slope(pre_act.reshape(tok_rows, -1))).astype(
        jnp.bfloat16
    )
    grad_cols = act_grad.reshape(tok_rows, col_count, block_size)

    def backward_step(running, shard_blocks, first_block):
        indices = lax.dynamic_slice_in_dim(all_indices, first_block, shard_blocks.shape[0], 0)
        cols_in = jnp.take(grad_cols, indices[:, 1], axis=1)
        product = jnp.einsum(
            "tbn,bkn->tbk", cols_in, shard_blocks, preferred_element_type=jnp.float32
        )
        return running.at[:, indices[:, 0]].add(product)

    back_zero = jnp.zeros((tok_rows, row_count, block_size), jnp.float32)
    input_grad = in_groups(
        backward_step, back_zero, lax.all_gather(own_blocks, "fsdp", axis=0, tiled=True)
    )
    input_grad = input_grad.astype(jnp.bfloat16).reshape(
        micro_count, activations.shape[2], activations.shape[3]
    )
    ordered = jnp.take(input_grad, order, axis=0)
    received = passed_along(ordered, "section", -1)
    indices = all_indices
    rows_in = jnp.take(features, indices[:, 0], axis=1)
    cols_in = jnp.take(grad_cols, indices[:, 1], axis=1)
    owned_grads = lax.psum_scatter(
        jnp.einsum("tbk,tbn->bkn", rows_in, cols_in, preferred_element_type=jnp.float32),
        "fsdp",
        scatter_dimension=0,
        tiled=True,
    )
    summed = lax.psum(owned_grads, "dp")
    grad_scale = 1.0 / math.sqrt(tok_rows * lax.axis_size("fsdp") * lax.axis_size("dp"))
    return (received[None], (summed * grad_scale)[None])


def solution(mesh):
    in_specs = (
        P("section", None, ("fsdp", "dp"), None),
        P("section", None, ("fsdp", "dp"), None),
        P("section", "fsdp", None, None),
        P("section", "fsdp", None),
        P(),
    )
    out_specs = (P("section", None, ("fsdp", "dp"), None), P("section", "fsdp", None, None))
    return jax.shard_map(local, mesh=mesh, in_specs=in_specs, out_specs=out_specs, check_vma=False)
```

profile of v0, /device:TPU:1, one launch (start us, length us, event | category | flops | bytes accessed | tf_op | source)
XLA Modules:
  0.0 444.8 jit_solution(14893785248069533942)
XLA Ops:
  7.2 0.0 all-gather.4.cloned.1.call-start
  7.2 0.7 all-gather.4.cloned.1.call-update
  7.9 0.0 reduce-scatter.2.cloned.1.call-start
  7.9 0.8 copy.31
  8.7 40.7 %all-gather = s32[1,128,2]{2,0,1:T(1,128)S(1)} all-gather(s32[1,4,2]{2,0,1:T(1,128)S(1)} %copy.31), channel_id=2, replica_groups=mesh['section'=2,'fsdp'=32,'dp'=4] {'fsdp'}, dimensions={1}, use_global_device_ids=true | all-gather | bytes 1056 | tf_op jit(solution)/shard_map/all_gather | solution.py:39
  49.4 0.1 copy.36
  49.5 1.6 reshape_squeeze.4
  51.1 0.4 copy.34
  51.5 5.9 %copy.41 = f32[16,8,112,128]{3,2,1,0:T(8,128)} copy(bf16[16,8,112,128]{3,1,2,0:T(8,128)(2,1)} %bitcast.51) | data formatting | bytes 11010048
  57.3 0.2 fusion.29
  57.5 3.1 gather_fusion.3
  60.6 0.2 and_reduce_fusion.1
  60.8 32.7 %all-gather.4.cloned.1.call-done = bf16[1,128,128,128]{3,2,0,1:T(8,128)(2,1)} async-done(((bf16[1,4,128,128]{3,2,0,1:T(8,128)(2,1)}), bf16[1,128,128,128]{3,2,0,1:T(8,128)(2,1)}) %all-gather.4.cloned.1.call-update) | async-done | bytes 4194320 | tf_op jit(solution)/shard_map/all_gather | solution.py:68
  93.5 3.9 broadcast_in_dim.90
  97.5 40.1 %while.26 = (s32[]{:T(128)}, f32[128,112,128]{2,0,1:T(8,128)}, s32[128,2]{0,1:T(2,128)S(1)}, bf16[128,128,128]{2,1,0:T(8,128)(2,1)}, bf16[128,28,128]{2,0,1:T(8,...) while((s32[]{:T(128)}, f32[128,112,128]{2,0,1:T(8,128)}, s32[128,2]{0,1:T(2,128)S(1)}, ...), condition=%wide.region_2.3_spmd, body=%wide.region_0.2_spmd.sunk | while | flops 135267712 | bytes 12588755 | solution.py:27
  97.5 0.1 constant_dynamic-slice_fusion.4
  97.5 1.7 gather_fusion
  99.2 2.0 fusion.43
  101.3 6.2 %scatter_fusion = f32[128,112,128]{2,0,1:T(8,128)} fusion(f32[128,112,128]{2,0,1:T(8,128)} %get-tuple-element.332, s32[32]{0:T(128)S(1)} %get-tuple-element.313, f32[32,128,128]{2,1,0:T(8,128)S(1)} %fusion.43), kind=kCustom, calls=%fused_computation.5.clone.1 | custom fusion | flops 524288 | bytes 6291584 | tf_op jit(solution)/shard_map/while/body/eval_jaxpr/scatter-add | solution.py:47
  107.5 0.1 constant_dynamic-slice_fusion.4
  107.6 1.7 gather_fusion
  109.3 2.0 fusion.43
  111.3 6.2 %scatter_fusion = f32[128,112,128]{2,0,1:T(8,128)} fusion(f32[128,112,128]{2,0,1:T(8,128)} %get-tuple-element.332, s32[32]{0:T(128)S(1)} %get-tuple-element.313, f32[32,128,128]{2,1,0:T(8,128)S(1)} %fusion.43), kind=kCustom, calls=%fused_computation.5.clone.1 | custom fusion | flops 524288 | bytes 6291584 | tf_op jit(solution)/shard_map/while/body/eval_jaxpr/scatter-add | solution.py:47
  117.5 0.1 constant_dynamic-slice_fusion.4
  117.6 1.7 gather_fusion
  119.3 2.0 fusion.43
  121.3 6.2 %scatter_fusion = f32[128,112,128]{2,0,1:T(8,128)} fusion(f32[128,112,128]{2,0,1:T(8,128)} %get-tuple-element.332, s32[32]{0:T(128)S(1)} %get-tuple-element.313, f32[32,128,128]{2,1,0:T(8,128)S(1)} %fusion.43), kind=kCustom, calls=%fused_computation.5.clone.1 | custom fusion | flops 524288 | bytes 6291584 | tf_op jit(solution)/shard_map/while/body/eval_jaxpr/scatter-add | solution.py:47
  127.5 0.1 constant_dynamic-slice_fusion.4
  127.6 1.7 gather_fusion
  129.3 2.0 fusion.43
  131.3 6.2 %scatter_fusion = f32[128,112,128]{2,0,1:T(8,128)} fusion(f32[128,112,128]{2,0,1:T(8,128)} %get-tuple-element.332, s32[32]{0:T(128)S(1)} %get-tuple-element.313, f32[32,128,128]{2,1,0:T(8,128)S(1)} %fusion.43), kind=kCustom, calls=%fused_computation.5.clone.1 | custom fusion | flops 524288 | bytes 6291584 | tf_op jit(solution)/shard_map/while/body/eval_jaxpr/scatter-add | solution.py:47
  137.5 8.5 %fusion.20 = bf16[128,112,128]{2,0,1:T(8,128)(2,1)} fusion(f32[128,112,128]{2,1,0:T(8,128)} %bitcast.49, f32[128,112,128]{2,0,1:T(8,128)} %get-tuple-element.190), kind=kLoop, calls=%fused_computation.38 | loop fusion | flops 16515072 | bytes 18350080 | tf_op jit(solution)/shard_map/convert_element_type | solution.py:53
  146.0 5.1 %gather_fusion.4 = bf16[128,128,128]{2,1,0:T(8,128)(2,1)} fusion(bf16[128,112,128]{2,0,1:T(8,128)(2,1)} %fusion.20, s32[1024]{0:T(1024)S(1)} %get-tuple-element.250), kind=kCustom, calls=%fused_computation.4 | custom fusion | bytes 8389120 | tf_op jit(solution)/shard_map/jit(_take)/gather | solution.py:77
  151.1 8.5 %fusion.21 = f32[128,128,128]{2,1,0:T(8,128)} fusion(bf16[128,128,128]{2,1,0:T(8,128)(2,1)} %gather_fusion.4, bf16[128,128,128]{2,1,0:T(8,128)(2,1)} %gather_fusion.3, pred[128]{0:T(512)(128)(4,1)S(1)} %get-tuple-element.223, pred[128]{0:T(512)(128)(4,1)S(1)} %get-tuple-element.222), kind=kOutput, calls=%fused_computation.39 | convolution fusion | flops 541065216 | bytes 16777472 | tf_op jit(solution)/shard_map/tbk,tbn->bkn/dot_general | solution.py:79
  159.7 0.2 all-reduce.2.cloned.1.call-start
  159.9 0.4 copy-done
  160.3 1.5 broadcast_in_dim.89
  161.8 45.7 %while.27 = (s32[]{:T(128)}, f32[128,28,128]{2,0,1:T(8,128)}, s32[128,2]{0,1:T(2,128)S(1)}, bf16[128,128,128]{2,1,0:T(8,128)(2,1)}, bf16[128,112,128]{2,0,1:T(8,...) while((s32[]{:T(128)}, f32[128,28,128]{2,0,1:T(8,128)}, s32[128,2]{0,1:T(2,128)S(1)}, ...), condition=%wide.region_5.6_spmd, body=%wide.region_3.5_spmd.sunk | while | flops 135267712 | bytes 12588755 | solution.py:27
  161.8 0.1 constant_dynamic-slice_fusion.5
  161.9 2.8 gather_fusion.1
  164.7 2.1 fusion.47
  166.8 6.4 %scatter_fusion.1 = f32[128,28,128]{2,0,1:T(8,128)} fusion(f32[128,28,128]{2,0,1:T(8,128)} %get-tuple-element.359, s32[32]{0:T(128)S(1)} %get-tuple-element.320, f32[32,128,128]{2,1,0:T(8,128)S(1)} %fusion.47), kind=kCustom, calls=%fused_computation.6.clone.1 | custom fusion | flops 524288 | bytes 6291584 | tf_op jit(solution)/shard_map/while/body/eval_jaxpr/scatter-add | solution.py:64
  173.2 0.1 constant_dynamic-slice_fusion.5
  173.3 2.8 gather_fusion.1
  176.1 2.1 fusion.47
  178.3 6.5 %scatter_fusion.1 = f32[128,28,128]{2,0,1:T(8,128)} fusion(f32[128,28,128]{2,0,1:T(8,128)} %get-tuple-element.359, s32[32]{0:T(128)S(1)} %get-tuple-element.320, f32[32,128,128]{2,1,0:T(8,128)S(1)} %fusion.47), kind=kCustom, calls=%fused_computation.6.clone.1 | custom fusion | flops 524288 | bytes 6291584 | tf_op jit(solution)/shard_map/while/body/eval_jaxpr/scatter-add | solution.py:64
  184.7 0.1 constant_dynamic-slice_fusion.5
  184.8 2.8 gather_fusion.1
  187.6 2.1 fusion.47
  189.8 6.3 %scatter_fusion.1 = f32[128,28,128]{2,0,1:T(8,128)} fusion(f32[128,28,128]{2,0,1:T(8,128)} %get-tuple-element.359, s32[32]{0:T(128)S(1)} %get-tuple-element.320, f32[32,128,128]{2,1,0:T(8,128)S(1)} %fusion.47), kind=kCustom, calls=%fused_computation.6.clone.1 | custom fusion | flops 524288 | bytes 6291584 | tf_op jit(solution)/shard_map/while/body/eval_jaxpr/scatter-add | solution.py:64
  196.1 0.1 constant_dynamic-slice_fusion.5
  196.1 2.9 gather_fusion.1
  199.1 2.1 fusion.47
  201.2 6.3 %scatter_fusion.1 = f32[128,28,128]{2,0,1:T(8,128)} fusion(f32[128,28,128]{2,0,1:T(8,128)} %get-tuple-element.359, s32[32]{0:T(128)S(1)} %get-tuple-element.320, f32[32,128,128]{2,1,0:T(8,128)S(1)} %fusion.47), kind=kCustom, calls=%fused_computation.6.clone.1 | custom fusion | flops 524288 | bytes 6291584 | tf_op jit(solution)/shard_map/while/body/eval_jaxpr/scatter-add | solution.py:64
  207.5 1.6 convert_element_type.17
  209.1 0.6 copy.37
  209.8 0.5 reshape.37
  210.3 0.6 gather_fusion.2
  210.9 0.2 broadcast_select_fusion
  211.0 1.3 collective-permute-start
  212.3 172.1 %reduce-scatter.2.cloned.1.call-done = f32[4,128,128]{2,1,0:T(8,128)} async-done(((f32[128,128,128]{2,1,0:T(8,128)}), f32[4,128,128]{2,1,0:T(8,128)}) %reduce-scatter.2.cloned.1.call-update) | async-done | bytes 262160 | tf_op jit(solution)/shard_map/reduce_scatter | solution.py:78
  384.5 51.2 %all-reduce.2.cloned.1.call-done = f32[4,128,128]{2,1,0:T(8,128)} async-done(((f32[4,128,128]{2,1,0:T(8,128)}), f32[4,128,128]{2,1,0:T(8,128)}) %all-reduce.2.cloned.1.call-update) | async-done | bytes 262160 | tf_op jit(solution)/shard_map/psum | solution.py:84
  435.7 1.7 multiply_bitcast_fusion
  437.3 0.9 copy.61
  (32 shorter events, 0.3 us)
Async XLA Ops:
  7.2 86.3 %all-gather.4.cloned.1.call-start = ((), (), s32[]{:S(2)}) async-start(), calls=%async_computation.3 | async-start | bytes 4325376 | tf_op jit(solution)/shard_map/all_gather | solution.py:68
  7.9 376.5 %reduce-scatter.2.cloned.1.call-start = ((), (), s32[]{:S(2)}) async-start(), calls=%async_computation.1 | async-start | bytes 8650752 | tf_op jit(solution)/shard_map/reduce_scatter | solution.py:78
  159.6 0.7 copy-start
  159.7 276.0 %all-reduce.2.cloned.1.call-start = ((), (), s32[]{:S(2)}) async-start(), calls=%async_computation.2 | async-start | bytes 524288 | tf_op jit(solution)/shard_map/psum | solution.py:84
  211.0 173.4 %collective-permute-start = (bf16[4,32,3584]{2,1,0:T(8,128)(2,1)S(1)}, bf16[4,32,3584]{2,1,0:T(8,128)(2,1)S(1)}, u32[]{:S(2)}, u32[]{:S(2)}) collective-permute-start(bf16[4,32,3584]{2,1,0:T(8,128)(2,1)S(1)} %broadcast_select_fusion), channel_id=1, source_target_pairs={{128,0},{129,1},{130,2},{131,3},{132,4},{133,5},{134,6},{135,7},{1... | collective-permute-start | bytes 2752520 | tf_op jit(solution)/shard_map/ppermute | solution.py:11
Sparse Core Ops, SparseCore 0:
  10.6 82.8 all-gather.3
  159.8 224.6 reduce-scatter.1
  387.3 48.3 all-reduce.1
where the time goes:
time: 447 us; the launch traced here: 445 us
  waiting for transfers between devices  257 us (57%)
  other arithmetic  62.9 us (14%)
  local copies, waits for them, and re-layouts  43.9 us (10%)
  blocking collectives  40.7 us (9%)
  matrix products  25.1 us (6%)
  between operations  13.8 us (3%)
    reduce_scatter x1, waiting for transfers between devices, local(): lax.psum_scatter(jnp.einsum('tbk,tbn->bkn', rows_in, cols_in, preferred_e...  172 us
    psum x1, waiting for transfers between devices, local(): summed = lax.psum(owned_grads, 'dp')  51.2 us
    all_gather x1, blocking collectives, local(): all_indices = lax.all_gather(pattern[0], 'fsdp', axis=0, tiled=True)  40.7 us
    all_gather x1, waiting for transfers between devices, local(): lax.all_gather(own_blocks, 'fsdp', axis=0, tiled=True)  32.7 us
    scatter-add x4, other arithmetic, backward_step(): return running.at[:, indices[:, 0]].add(product)  25.5 us
    scatter-add x4, other arithmetic, forward_step(): return running.at[:, indices[:, 1]].add(product)  24.8 us
    gather x4, local copies, waits for them, and re-layouts, backward_step(): cols_in = jnp.take(grad_cols, indices[:, 1], axis=1)  11.3 us
  transfers between devices with their start and end apart: 4, of which 3 were waited for; matrix products, arithmetic and copies ran while one was open for 14% of the time, Pallas kernels for 0%

commit v1 on v0

--- a/solution.py
+++ b/solution.py
@@ -65,7 +65,11 @@
 
     back_zero = jnp.zeros((tok_rows, row_count, block_size), jnp.float32)
     input_grad = in_groups(
-        backward_step, back_zero, lax.all_gather(own_blocks, "fsdp", axis=0, tiled=True)
+        backward_step,
+        back_zero,
+        jnp.concatenate(
+            lax.all_to_all(jnp.stack([own_blocks] * lax.axis_size("fsdp")), "fsdp", 0, 0), axis=0
+        ),
     )
     input_grad = input_grad.astype(jnp.bfloat16).reshape(
         micro_count, activations.shape[2], activations.shape[3]

time: 447 us -> 489 us (1.094)
  waiting for transfers between devices: 257 us -> 285 us
  local copies, waits for them, and re-layouts: 43.9 us -> 51 us
  starting transfers between devices: 1.59 us -> 7.47 us
    all_to_all x0 -> x1, waiting for transfers between devices: none -> 118 us  [local(): lax.all_to_all(jnp.stack([own_blocks] * lax.axis_size('fsdp')), 'fsdp', 0...]
    reduce_scatter x1, waiting for transfers between devices: 172 us -> 82.3 us  [local(): lax.psum_scatter(jnp.einsum('tbk,tbn->bkn', rows_in, cols_in, preferred_e...]
    all_to_all x0 -> x1, starting transfers between devices: none -> 5.88 us  [local(): lax.all_to_all(jnp.stack([own_blocks] * lax.axis_size('fsdp')), 'fsdp', 0...]
  transfers between devices with their start and end apart: 4 -> 5, of which waited for: 3 -> 4; matrix products, arithmetic and copies ran while one was open for 14% -> 15% of each run, Pallas kernels for 0% -> 0%
where the time goes in v1:
time: 489 us; the launch traced here: 487 us
  waiting for transfers between devices  285 us (58%)
  other arithmetic  62.9 us (13%)
  local copies, waits for them, and re-layouts  51 us (10%)
  blocking collectives  40.7 us (8%)
  matrix products  26.4 us (5%)
  between operations  13.9 us (3%)
  starting transfers between devices  7.47 us (2%)
    all_to_all x1, waiting for transfers between devices, local(): lax.all_to_all(jnp.stack([own_blocks] * lax.axis_size('fsdp')), 'fsdp', 0...  118 us
    reduce_scatter x1, waiting for transfers between devices, local(): lax.psum_scatter(jnp.einsum('tbk,tbn->bkn', rows_in, cols_in, preferred_e...  82.3 us
    psum x1, waiting for transfers between devices, local(): summed = lax.psum(owned_grads, 'dp')  51.3 us
    all_gather x1, blocking collectives, local(): all_indices = lax.all_gather(pattern[0], 'fsdp', axis=0, tiled=True)  40.7 us
    all_gather x1, waiting for transfers between devices, local(): lax.all_gather(own_blocks, 'fsdp', axis=0, tiled=True)  32.7 us
    scatter-add x4, other arithmetic, backward_step(): return running.at[:, indices[:, 0]].add(product)  25.6 us
    scatter-add x4, other arithmetic, forward_step(): return running.at[:, indices[:, 1]].add(product)  24.8 us
    gather x4, local copies, waits for them, and re-layouts, backward_step(): cols_in = jnp.take(grad_cols, indices[:, 1], axis=1)  14.9 us
  transfers between devices with their start and end apart: 5, of which 4 were waited for; matrix products, arithmetic and copies ran while one was open for 15% of the time, Pallas kernels for 0%

profile of v1, /device:TPU:1, one launch (start us, length us, event | category | flops | bytes accessed | tf_op | source)
XLA Modules:
  0.0 487.2 jit_solution(17720586900554729488)
XLA Ops:
  7.2 0.7 all-gather.4.cloned.1.call-update
  7.9 0.8 copy.31
  8.7 40.7 %all-gather = s32[1,128,2]{2,0,1:T(1,128)S(1)} all-gather(s32[1,4,2]{2,0,1:T(1,128)S(1)} %copy.31), channel_id=2, replica_groups=mesh['section'=2,'fsdp'=32,'dp'=4] {'fsdp'}, dimensions={1}, use_global_device_ids=true | all-gather | bytes 1056 | tf_op jit(solution)/shard_map/all_gather | solution.py:39
  49.5 1.6 reshape_squeeze.4
  51.1 0.4 copy.34
  51.5 5.9 %copy.41 = f32[16,8,112,128]{3,2,1,0:T(8,128)} copy(bf16[16,8,112,128]{3,1,2,0:T(8,128)(2,1)} %bitcast.53) | data formatting | bytes 11010048
  57.3 0.2 fusion.29
  57.5 3.1 gather_fusion.3
  60.6 0.2 and_reduce_fusion.1
  60.8 32.7 %all-gather.4.cloned.1.call-done = bf16[1,128,128,128]{3,2,0,1:T(8,128)(2,1)} async-done(((bf16[1,4,128,128]{3,2,0,1:T(8,128)(2,1)}), bf16[1,128,128,128]{3,2,0,1:T(8,128)(2,1)}) %all-gather.4.cloned.1.call-update) | async-done | bytes 4194320 | tf_op jit(solution)/shard_map/all_gather | solution.py:51
  93.5 3.9 broadcast_in_dim.90
  97.5 40.1 %while.26 = (s32[]{:T(128)}, f32[128,112,128]{2,0,1:T(8,128)}, s32[128,2]{0,1:T(2,128)S(1)}, bf16[128,128,128]{2,1,0:T(8,128)(2,1)}, bf16[128,28,128]{2,0,1:T(8,...) while((s32[]{:T(128)}, f32[128,112,128]{2,0,1:T(8,128)}, s32[128,2]{0,1:T(2,128)S(1)}, ...), condition=%wide.region_2.3_spmd, body=%wide.region_0.2_spmd.sunk | while | flops 135267712 | bytes 12588755 | solution.py:27
  97.5 0.1 constant_dynamic-slice_fusion.4
  97.5 1.7 gather_fusion
  99.2 2.0 fusion.43
  101.3 6.2 %scatter_fusion = f32[128,112,128]{2,0,1:T(8,128)} fusion(f32[128,112,128]{2,0,1:T(8,128)} %get-tuple-element.332, s32[32]{0:T(128)S(1)} %get-tuple-element.313, f32[32,128,128]{2,1,0:T(8,128)S(1)} %fusion.43), kind=kCustom, calls=%fused_computation.5.clone.1 | custom fusion | flops 524288 | bytes 6291584 | tf_op jit(solution)/shard_map/while/body/eval_jaxpr/scatter-add | solution.py:47
  107.5 0.1 constant_dynamic-slice_fusion.4
  107.6 1.7 gather_fusion
  109.3 2.0 fusion.43
  111.3 6.2 %scatter_fusion = f32[128,112,128]{2,0,1:T(8,128)} fusion(f32[128,112,128]{2,0,1:T(8,128)} %get-tuple-element.332, s32[32]{0:T(128)S(1)} %get-tuple-element.313, f32[32,128,128]{2,1,0:T(8,128)S(1)} %fusion.43), kind=kCustom, calls=%fused_computation.5.clone.1 | custom fusion | flops 524288 | bytes 6291584 | tf_op jit(solution)/shard_map/while/body/eval_jaxpr/scatter-add | solution.py:47
  117.5 0.1 constant_dynamic-slice_fusion.4
  117.6 1.7 gather_fusion
  119.3 2.0 fusion.43
  121.3 6.2 %scatter_fusion = f32[128,112,128]{2,0,1:T(8,128)} fusion(f32[128,112,128]{2,0,1:T(8,128)} %get-tuple-element.332, s32[32]{0:T(128)S(1)} %get-tuple-element.313, f32[32,128,128]{2,1,0:T(8,128)S(1)} %fusion.43), kind=kCustom, calls=%fused_computation.5.clone.1 | custom fusion | flops 524288 | bytes 6291584 | tf_op jit(solution)/shard_map/while/body/eval_jaxpr/scatter-add | solution.py:47
  127.5 0.1 constant_dynamic-slice_fusion.4
  127.6 1.7 gather_fusion
  129.3 2.0 fusion.43
  131.3 6.2 %scatter_fusion = f32[128,112,128]{2,0,1:T(8,128)} fusion(f32[128,112,128]{2,0,1:T(8,128)} %get-tuple-element.332, s32[32]{0:T(128)S(1)} %get-tuple-element.313, f32[32,128,128]{2,1,0:T(8,128)S(1)} %fusion.43), kind=kCustom, calls=%fused_computation.5.clone.1 | custom fusion | flops 524288 | bytes 6291584 | tf_op jit(solution)/shard_map/while/body/eval_jaxpr/scatter-add | solution.py:47
  137.5 8.4 %fusion.20 = bf16[128,112,128]{2,0,1:T(8,128)(2,1)} fusion(f32[128,112,128]{2,1,0:T(8,128)} %bitcast.51, f32[128,112,128]{2,0,1:T(8,128)} %get-tuple-element.190), kind=kLoop, calls=%fused_computation.38 | loop fusion | flops 16515072 | bytes 18350080 | tf_op jit(solution)/shard_map/convert_element_type | solution.py:53
  146.0 5.1 %gather_fusion.4 = bf16[128,128,128]{2,1,0:T(8,128)(2,1)} fusion(bf16[128,112,128]{2,0,1:T(8,128)(2,1)} %fusion.20, s32[1024]{0:T(1024)S(1)} %get-tuple-element.250), kind=kCustom, calls=%fused_computation.4 | custom fusion | bytes 8389120 | tf_op jit(solution)/shard_map/jit(_take)/gather | solution.py:81
  151.1 8.5 %fusion.21 = f32[128,128,128]{2,1,0:T(8,128)} fusion(bf16[128,128,128]{2,1,0:T(8,128)(2,1)} %gather_fusion.4, bf16[128,128,128]{2,1,0:T(8,128)(2,1)} %gather_fusion.3, pred[128]{0:T(512)(128)(4,1)S(1)} %get-tuple-element.223, pred[128]{0:T(512)(128)(4,1)S(1)} %get-tuple-element.222), kind=kOutput, calls=%fused_computation.39 | convolution fusion | flops 541065216 | bytes 16777472 | tf_op jit(solution)/shard_map/tbk,tbn->bkn/dot_general | solution.py:83
  159.6 0.9 copy-done
  160.5 3.0 stack.3
  163.5 5.9 %all-to-all-start = ((bf16[32,4,128,128]{3,2,1,0:T(8,128)(2,1)}), bf16[32,4,128,128]{3,2,1,0:T(8,128)(2,1)}, u32[]{:S(2)}, u32[]{:S(2)}) async-start(bf16[32,4,128,128]{3,2,1,0:T(8,128)(2,1)} %stack.3), calls=%async_computation | async-start | bytes 8388608 | tf_op jit(solution)/shard_map/all_to_all | solution.py:71
  169.4 0.2 all-reduce.2.cloned.1.call-start
  169.6 117.8 %all-to-all-done = bf16[32,4,128,128]{3,2,1,0:T(8,128)(2,1)} async-done(((bf16[32,4,128,128]{3,2,1,0:T(8,128)(2,1)}), bf16[32,4,128,128]{3,2,1,0:T(8,128)(2,1)}, u32[]{:S(2)}, u32[]{:S(2)}) %all-to-all-start) | async-done | bytes 4194336 | tf_op jit(solution)/shard_map/all_to_all | solution.py:71
  287.5 1.5 broadcast_in_dim.89
  289.0 50.6 %while.27 = (s32[]{:T(128)}, f32[128,28,128]{2,0,1:T(8,128)}, s32[128,2]{0,1:T(2,128)S(1)}, bf16[128,128,128]{2,1,0:T(8,128)(2,1)}, bf16[128,112,128]{2,0,1:T(8,...) while((s32[]{:T(128)}, f32[128,28,128]{2,0,1:T(8,128)}, s32[128,2]{0,1:T(2,128)S(1)}, ...), condition=%wide.region_5.6_spmd, body=%wide.region_3.5_spmd.sunk | while | flops 135267712 | bytes 12588755 | solution.py:27
  289.0 0.1 constant_dynamic-slice_fusion.5
  289.1 3.7 gather_fusion.1
  292.8 2.4 fusion.47
  295.2 6.5 %scatter_fusion.1 = f32[128,28,128]{2,0,1:T(8,128)} fusion(f32[128,28,128]{2,0,1:T(8,128)} %get-tuple-element.359, s32[32]{0:T(128)S(1)} %get-tuple-element.320, f32[32,128,128]{2,1,0:T(8,128)S(1)} %fusion.47), kind=kCustom, calls=%fused_computation.6.clone.1 | custom fusion | flops 524288 | bytes 6291584 | tf_op jit(solution)/shard_map/while/body/eval_jaxpr/scatter-add | solution.py:64
  301.7 0.1 constant_dynamic-slice_fusion.5
  301.8 3.7 gather_fusion.1
  305.5 2.4 fusion.47
  308.0 6.2 %scatter_fusion.1 = f32[128,28,128]{2,0,1:T(8,128)} fusion(f32[128,28,128]{2,0,1:T(8,128)} %get-tuple-element.359, s32[32]{0:T(128)S(1)} %get-tuple-element.320, f32[32,128,128]{2,1,0:T(8,128)S(1)} %fusion.47), kind=kCustom, calls=%fused_computation.6.clone.1 | custom fusion | flops 524288 | bytes 6291584 | tf_op jit(solution)/shard_map/while/body/eval_jaxpr/scatter-add | solution.py:64
  314.2 0.1 constant_dynamic-slice_fusion.5
  314.3 3.8 gather_fusion.1
  318.0 2.4 fusion.47
  320.5 6.5 %scatter_fusion.1 = f32[128,28,128]{2,0,1:T(8,128)} fusion(f32[128,28,128]{2,0,1:T(8,128)} %get-tuple-element.359, s32[32]{0:T(128)S(1)} %get-tuple-element.320, f32[32,128,128]{2,1,0:T(8,128)S(1)} %fusion.47), kind=kCustom, calls=%fused_computation.6.clone.1 | custom fusion | flops 524288 | bytes 6291584 | tf_op jit(solution)/shard_map/while/body/eval_jaxpr/scatter-add | solution.py:64
  327.0 0.1 constant_dynamic-slice_fusion.5
  327.1 3.7 gather_fusion.1
  330.8 2.4 fusion.47
  333.2 6.4 %scatter_fusion.1 = f32[128,28,128]{2,0,1:T(8,128)} fusion(f32[128,28,128]{2,0,1:T(8,128)} %get-tuple-element.359, s32[32]{0:T(128)S(1)} %get-tuple-element.320, f32[32,128,128]{2,1,0:T(8,128)S(1)} %fusion.47), kind=kCustom, calls=%fused_computation.6.clone.1 | custom fusion | flops 524288 | bytes 6291584 | tf_op jit(solution)/shard_map/while/body/eval_jaxpr/scatter-add | solution.py:64
  339.6 1.7 convert_element_type.17
  341.2 0.6 copy.37
  341.9 0.5 reshape.42
  342.3 0.6 gather_fusion.2
  343.0 0.2 broadcast_select_fusion
  343.1 1.3 collective-permute-start
  344.4 82.3 %reduce-scatter.2.cloned.1.call-done = f32[4,128,128]{2,1,0:T(8,128)} async-done(((f32[128,128,128]{2,1,0:T(8,128)}), f32[4,128,128]{2,1,0:T(8,128)}) %reduce-scatter.2.cloned.1.call-update) | async-done | bytes 262160 | tf_op jit(solution)/shard_map/reduce_scatter | solution.py:82
  426.8 51.3 %all-reduce.2.cloned.1.call-done = f32[4,128,128]{2,1,0:T(8,128)} async-done(((f32[4,128,128]{2,1,0:T(8,128)}), f32[4,128,128]{2,1,0:T(8,128)}) %all-reduce.2.cloned.1.call-update) | async-done | bytes 262160 | tf_op jit(solution)/shard_map/psum | solution.py:88
  478.1 1.7 multiply_bitcast_fusion
  479.8 0.9 copy.61
  (37 shorter events, 0.4 us)
Async XLA Ops:
  7.2 86.3 %all-gather.4.cloned.1.call-start = ((), (), s32[]{:S(2)}) async-start(), calls=%async_computation.4 | async-start | bytes 4325376 | tf_op jit(solution)/shard_map/all_gather | solution.py:51
  7.9 418.9 %reduce-scatter.2.cloned.1.call-start = ((), (), s32[]{:S(2)}) async-start(), calls=%async_computation.2 | async-start | bytes 8650752 | tf_op jit(solution)/shard_map/reduce_scatter | solution.py:82
  159.6 0.9 copy-start
  163.5 6.1 %copy-start.1 = (s32[4]{0:T(128)S(1)}, s32[4]{0:T(128)}, u32[]{:S(2)}) copy-start(s32[4]{0:T(128)} %param.13) | copy-start | bytes 52
  163.5 124.0 %all-to-all-start = ((bf16[32,4,128,128]{3,2,1,0:T(8,128)(2,1)}), bf16[32,4,128,128]{3,2,1,0:T(8,128)(2,1)}, u32[]{:S(2)}, u32[]{:S(2)}) async-start(bf16[32,4,128,128]{3,2,1,0:T(8,128)(2,1)} %stack.3), calls=%async_computation | async-start | bytes 8388608 | tf_op jit(solution)/shard_map/all_to_all | solution.py:71
  169.4 308.7 %all-reduce.2.cloned.1.call-start = ((), (), s32[]{:S(2)}) async-start(), calls=%async_computation.3 | async-start | bytes 524288 | tf_op jit(solution)/shard_map/psum | solution.py:88
  343.1 83.7 %collective-permute-start = (bf16[4,32,3584]{2,1,0:T(8,128)(2,1)S(1)}, bf16[4,32,3584]{2,1,0:T(8,128)(2,1)S(1)}, u32[]{:S(2)}, u32[]{:S(2)}) collective-permute-start(bf16[4,32,3584]{2,1,0:T(8,128)(2,1)S(1)} %broadcast_select_fusion), channel_id=1, source_target_pairs={{128,0},{129,1},{130,2},{131,3},{132,4},{133,5},{134,6},{135,7},{1... | collective-permute-start | bytes 2752520 | tf_op jit(solution)/shard_map/ppermute | solution.py:11
Sparse Core Ops, SparseCore 0:
  10.6 82.8 all-gather.3
  159.7 266.9 reduce-scatter.1
  429.6 48.4 all-reduce.1
